TPU v7x, 256 devices: a whole 4x4x8 slice. The times are simulated.
256 devices in a mesh: gx: 32 (over y_hi, z, core), gy: 8 (over y_lo, x).
Axes of the slice: x: 4, y: 4 (y_hi: 2, y_lo: 2; y = y_hi * 2 + y_lo), z: 8, core: 2. Of those that a mesh axis runs over, the one named last changes fastest.
Arguments:
- positions: float32 [3, 524288], P(None, ('gx', 'gy')), may hold values from 0 to 6
- features: bfloat16 [64, 524288], P(None, ('gx', 'gy')), may hold values from -6 to 6
- halo_lists: int32 [2, 393216], P(None, ('gx', 'gy')), may hold values from 0 to 2047
- local_pairs: int32 [4, 1572864], P(None, ('gx', 'gy')), may hold values from 0 to 2047, as said below
- cross_x: int32 [4, 524288], P(None, ('gx', 'gy')), may hold values from 0 to 2047, as said below
- cross_y: int32 [4, 524288], P(None, ('gx', 'gy')), may hold values from 0 to 2047, as said below
- pair_counts: int32 [256, 3], P(('gx', 'gy')), may hold values from 256 to 6144, as said below
- w_rbf: bfloat16 [8, 256], replicated, may hold values from -2 to 2
- w_src: bfloat16 [64, 256], replicated, may hold values from -0.75 to 0.75
- w_dst: bfloat16 [64, 256], replicated, may hold values from -0.75 to 0.75
- species_src: bfloat16 [4, 256], replicated, may hold values from -3 to 3
- species_dst: bfloat16 [4, 256], replicated, may hold values from -3 to 3
- w_hidden: bfloat16 [256, 256], replicated, may hold values from -0.375 to 0.375
- w_latent: bfloat16 [256, 64], replicated, may hold values from -0.375 to 0.375
- w_energy: float32 [64], replicated, may hold values from -0.75 to 0.75
Outputs:
- energy: float32 [1], replicated
- forces: float32 [3, 524288], P(None, ('gx', 'gy'))
- feature_grads: float32 [64, 524288], P(None, ('gx', 'gy'))
Inputs may be any that keep to these rules, and one draw needn't show every extreme that they name: `local_pairs`: rows 0 and 1 are different atoms of the block, below 2048; rows 2 and 3 are species below 4. `cross_x`: row 0 an atom below 2048, row 1 a slot below 1536, rows 2 and 3 species below 4. `cross_y`: row 0 an atom below 2048, row 1 a slot below 1536, rows 2 and 3 species below 4. `pair_counts`: column 0 counts live slots of local_pairs (at most 6144), columns 1 and 2 those of cross_x and cross_y (at most 2048); live slots come first; some device is full in each column.
All inputs are finite; a program needn't handle non-finite values.
Results may differ from a plain program's by a relative error of at most 0.0095.
Values may be sent and summed in bfloat16 or wider, within the bound.
A program may use at most 64 MiB of HBM per device.

v0:
```python
import jax
import jax.numpy as jnp
from jax import lax
from jax.sharding import PartitionSpec as P

BLOCK = 512
cutoff_radius = 6.0
block_edge = 6.0
softening = 0.1


def shifted(array, axis, by):
    length = lax.axis_size(axis)
    return lax.ppermute(array, axis, [(i, (i + by) % length) for i in range(length)])


def pair_energy(
    src_pos, src_feat, dst_pos, dst_feat, spec_src, spec_dst, live_mask, offset, weights
):
    w_rbf, w_src, w_dst, species_src, species_dst, w_hidden, w_latent, w_energy = weights
    displace = dst_pos + offset[:, None] - src_pos
    radius = jnp.sqrt(jnp.sum(displace * displace, axis=0) + softening)
    orders = jnp.arange(1, w_rbf.shape[0] + 1).astype(jnp.float32)[:, None]
    basis = (jnp.sin(orders * (jnp.pi / cutoff_radius) * radius[None, :]) / radius[None, :]).astype(
        jnp.bfloat16
    )
    kinds = jnp.arange(species_src.shape[0], dtype=jnp.int32)[:, None]
    onehot_src = (spec_src[None, :] == kinds).astype(jnp.bfloat16)
    onehot_dst = (spec_dst[None, :] == kinds).astype(jnp.bfloat16)
    pre = jnp.dot(w_rbf.T, basis, preferred_element_type=jnp.float32)
    pre = pre + jnp.dot(w_src.T, src_feat.astype(jnp.bfloat16), preferred_element_type=jnp.float32)
    pre = pre + jnp.dot(w_dst.T, dst_feat.astype(jnp.bfloat16), preferred_element_type=jnp.float32)
    pre = pre + jnp.dot(species_src.T, onehot_src, preferred_element_type=jnp.float32)
    pre = pre + jnp.dot(species_dst.T, onehot_dst, preferred_element_type=jnp.float32)
    hidden = jax.nn.silu(pre).astype(jnp.bfloat16)
    second = jax.nn.silu(jnp.dot(w_hidden.T, hidden, preferred_element_type=jnp.float32)).astype(
        jnp.bfloat16
    )
    latent = jnp.dot(w_latent.T, second, preferred_element_type=jnp.float32)
    ratio = jnp.minimum(radius / cutoff_radius, 1.0)
    envelope = (1.0 - ratio**2) ** 2
    scores = jnp.dot(w_energy, latent, precision=lax.Precision.HIGHEST)
    return jnp.sum(envelope * scores * live_mask)


def block_grads(
    src_pos, src_feat, dst_pos, dst_feat, spec_src, spec_dst, live_mask, offset, weights
):

    def energy_of(pos_one, feat_one, pos_two, feat_two):
        return pair_energy(
            pos_one, feat_one, pos_two, feat_two, spec_src, spec_dst, live_mask, offset, weights
        )

    energy, pullback = jax.vjp(
        energy_of, src_pos, src_feat.astype(jnp.float32), dst_pos, dst_feat.astype(jnp.float32)
    )
    return (energy, pullback(jnp.ones_like(energy)))


def to_blocks(array):
    count = array.shape[-1] // BLOCK
    if array.ndim == 1:
        return array.reshape(count, BLOCK)
    return jnp.moveaxis(array.reshape(array.shape[0], count, BLOCK), 1, 0)


def from_blocks(array):
    return jnp.moveaxis(array, 0, 1).reshape(array.shape[1], -1)


def run_edges(src_pos, src_feat, dst_pos, dst_feat, spec_src, spec_dst, live_mask, offset, weights):
    inputs = (src_pos, src_feat, dst_pos, dst_feat, spec_src, spec_dst, live_mask)

    def visit(total, blocks):
        energy, grads = block_grads(*blocks, offset, weights)
        return (total + energy, grads)

    total, grads = lax.scan(
        visit, jnp.zeros((), jnp.float32), tuple((to_blocks(item) for item in inputs))
    )
    return (total, tuple((from_blocks(item) for item in grads)))


def on_device(
    positions,
    features,
    halo_lists,
    local_pairs,
    cross_x,
    cross_y,
    pair_counts,
    w_rbf,
    w_src,
    w_dst,
    species_src,
    species_dst,
    w_hidden,
    w_latent,
    w_energy,
):
    weights = (w_rbf, w_src, w_dst, species_src, species_dst, w_hidden, w_latent, w_energy)
    atoms = positions.shape[1]
    halo_size = halo_lists.shape[1]
    width = features.shape[0]
    list_x = halo_lists[0]
    list_y = halo_lists[1]
    got_pos_x = shifted(positions[:, list_x], "gx", -1)
    got_feat_x = shifted(features[:, list_x], "gx", -1)
    got_pos_y = shifted(positions[:, list_y], "gy", -1)
    got_feat_y = shifted(features[:, list_y], "gy", -1)
    zero_off = jnp.zeros((3,), jnp.float32)
    off_x = jnp.array([block_edge, 0.0, 0.0], jnp.float32)
    off_y = jnp.array([0.0, block_edge, 0.0], jnp.float32)
    counts = pair_counts[0]
    slots_loc = jnp.arange(local_pairs.shape[1], dtype=jnp.int32)
    slots_cross = jnp.arange(cross_x.shape[1], dtype=jnp.int32)
    live_loc = (slots_loc < counts[0]).astype(jnp.float32)
    flag_x = (slots_cross < counts[1]).astype(jnp.int32)
    flag_y = (slots_cross < counts[2]).astype(jnp.int32)
    source, target = (local_pairs[0], local_pairs[1])
    energy_loc, grads = run_edges(
        positions[:, source],
        features[:, source],
        positions[:, target],
        features[:, target],
        local_pairs[2],
        local_pairs[3],
        live_loc,
        zero_off,
        weights,
    )
    grad_pos = (
        jnp.zeros((3, atoms), jnp.float32).at[:, source].add(grads[0]).at[:, target].add(grads[2])
    )
    grad_feat = (
        jnp.zeros((width, atoms), jnp.float32)
        .at[:, source]
        .add(grads[1])
        .at[:, target]
        .add(grads[3])
    )
    source_x, slot_x = (cross_x[0], cross_x[1])
    src_pos_x = positions[:, source_x]
    src_feat_x = features[:, source_x]
    energy_x, grads_x = run_edges(
        src_pos_x,
        src_feat_x,
        got_pos_x[:, slot_x],
        got_feat_x[:, slot_x],
        cross_x[2],
        cross_x[3],
        flag_x.astype(jnp.float32),
        off_x,
        weights,
    )
    grad_pos = grad_pos.at[:, source_x].add(grads_x[0])
    grad_feat = grad_feat.at[:, source_x].add(grads_x[1])
    source_y, slot_y = (cross_y[0], cross_y[1])
    src_pos_y = positions[:, source_y]
    src_feat_y = features[:, source_y]
    energy_y, grads_y = run_edges(
        src_pos_y,
        src_feat_y,
        got_pos_y[:, slot_y],
        got_feat_y[:, slot_y],
        cross_y[2],
        cross_y[3],
        flag_y.astype(jnp.float32),
        off_y,
        weights,
    )
    grad_pos = grad_pos.at[:, source_y].add(grads_y[0])
    grad_feat = grad_feat.at[:, source_y].add(grads_y[1])
    lent_pos_x = jnp.zeros((3, halo_size), jnp.float32).at[:, slot_x].add(grads_x[2])
    lent_feat_x = jnp.zeros((width, halo_size), jnp.float32).at[:, slot_x].add(grads_x[3])
    back_pos_x, back_feat_x = shifted((lent_pos_x, lent_feat_x), "gx", 1)
    lent_pos_y = jnp.zeros((3, halo_size), jnp.float32).at[:, slot_y].add(grads_y[2])
    lent_feat_y = jnp.zeros((width, halo_size), jnp.float32).at[:, slot_y].add(grads_y[3])
    back_pos_y, back_feat_y = shifted((lent_pos_y, lent_feat_y), "gy", 1)
    grad_pos = grad_pos.at[:, list_x].add(back_pos_x).at[:, list_y].add(back_pos_y)
    grad_feat = grad_feat.at[:, list_x].add(back_feat_x).at[:, list_y].add(back_feat_y)
    total = lax.psum(energy_loc + energy_x + energy_y, ("gx", "gy"))
    atoms_all = atoms * lax.axis_size("gx") * lax.axis_size("gy")
    energy = (total / atoms_all).reshape(1)
    return (energy, -grad_pos, grad_feat)


def solution(mesh):
    return jax.shard_map(
        on_device,
        mesh=mesh,
        in_specs=(
            P(None, ("gx", "gy")),
            P(None, ("gx", "gy")),
            P(None, ("gx", "gy")),
            P(None, ("gx", "gy")),
            P(None, ("gx", "gy")),
            P(None, ("gx", "gy")),
            P(("gx", "gy"), None),
            P(),
            P(),
            P(),
            P(),
            P(),
            P(),
            P(),
            P(),
        ),
        out_specs=(P(), P(None, ("gx", "gy")), P(None, ("gx", "gy"))),
        check_vma=False,
    )
```

profile of v0, /device:TPU:1, one launch (start us, length us, event | category | flops | bytes accessed | tf_op | source)
XLA Modules:
  0.0 808.2 jit_solution(13375963660446118232)
XLA Ops:
  2.7 2.6 gather_fusion.4
  5.5 3.3 collective-permute-start
  9.1 4.0 gather_fusion.8
  13.2 6.3 collective-permute-start.1
  19.4 2.6 gather_fusion.10
  22.9 2.6 collective-permute-start.2
  25.5 4.0 gather_fusion.14
  34.0 21.1 %gather_fusion.1 = f32[6144,3]{1,0:T(8,128)} fusion(f32[3,2048]{0,1:T(8,128)S(1)} %copy.90, s32[6144]{0:T(1024)S(1)} %broadcast_clamp_fusion), kind=kCustom, calls=%fused_computation.1 | custom fusion | bytes 172032 | tf_op jit(solution)/shard_map/gather | solution.py:123
  55.0 22.0 %gather_fusion.2 = bf16[6144,64]{1,0:T(8,128)(2,1)} fusion(bf16[64,2048]{0,1:T(8,128)(2,1)S(1)} %copy.94, s32[6144]{0:T(1024)S(1)} %broadcast_clamp_fusion), kind=kCustom, calls=%fused_computation.2 | custom fusion | bytes 1597440 | tf_op jit(solution)/shard_map/gather | solution.py:124
  77.1 20.9 %gather_fusion = f32[6144,3]{1,0:T(8,128)} fusion(f32[3,2048]{0,1:T(8,128)S(1)} %copy.90, s32[6144]{0:T(1024)S(1)} %broadcast_clamp_fusion.1), kind=kCustom, calls=%fused_computation | custom fusion | bytes 172032 | tf_op jit(solution)/shard_map/gather | solution.py:125
  98.0 22.1 %gather_fusion.3 = bf16[6144,64]{1,0:T(8,128)(2,1)} fusion(bf16[64,2048]{0,1:T(8,128)(2,1)S(1)} %copy.94, s32[6144]{0:T(1024)S(1)} %broadcast_clamp_fusion.1), kind=kCustom, calls=%fused_computation.3 | custom fusion | bytes 1597440 | tf_op jit(solution)/shard_map/gather | solution.py:126
  120.1 7.6 gather_fusion.6
  127.6 6.2 gather_fusion.7
  133.8 7.6 gather_fusion.12
  141.4 8.0 gather_fusion.13
  149.4 3.0 copy.91
  152.4 3.1 copy.93
  156.9 2.5 copy.97
  164.0 7.6 gather_fusion.5
  174.2 7.6 gather_fusion.11
  183.4 6.2 gather_fusion.9
  190.0 35.0 %while.57 = (s32[]{:T(128)}, f32[]{:T(128)}, f32[4,3,512]{2,1,0:T(4,128)S(1)}, f32[4,64,512]{2,1,0:T(8,128)S(1)}, f32[4,3,512]{2,1,0:T(4,128)S(1)}, /*index=5*/f...) while((s32[]{:T(128)}, f32[]{:T(128)}, ...), condition=%wide.region_11.12_spmd.clone, body=%wide.region_6.11_spmd.sunk.clone.sunk | while | flops 246597152 | bytes 9618793 | solution.py:79
  191.7 2.0 convolution_bitcast_fusion.14
  200.4 2.0 convolution_bitcast_fusion.14
  202.4 1.6 fusion.381
  209.2 2.0 convolution_bitcast_fusion.14
  211.1 1.6 fusion.381
  217.9 2.0 convolution_bitcast_fusion.14
  225.0 6.2 gather_fusion.15
  232.4 37.8 %while.58 = (s32[]{:T(128)}, f32[]{:T(128)}, f32[4,3,512]{2,1,0:T(4,128)S(1)}, f32[4,64,512]{2,1,0:T(8,128)S(1)}, f32[4,3,512]{2,1,0:T(4,128)S(1)}, /*index=5*/f...) while((s32[]{:T(128)}, f32[]{:T(128)}, ...), condition=%wide.region_17.18_spmd.clone, body=%wide.region_12.17_spmd.sunk.clone.sunk | while | flops 246597152 | bytes 9619301 | solution.py:79
  234.1 2.0 convolution_bitcast_fusion.16
  236.1 1.6 fusion.411
  243.5 2.0 convolution_bitcast_fusion.16
  245.5 1.6 fusion.411
  253.0 2.0 convolution_bitcast_fusion.16
  255.0 1.6 fusion.411
  262.4 2.0 convolution_bitcast_fusion.16
  272.2 12.0 %scatter_custom_fusion.12 = f32[64,1536]{0,1:T(8,128)S(1)} fusion(s32[2048]{0:T(1024)S(1)} %bitcast.614, f32[2048,64]{1,0:T(8,128)} %copy.137, f32[]{:T(128)} %constant.151.clone.1), kind=kCustom, calls=%fused_computation.294 | custom fusion | flops 131072 | bytes 393728 | tf_op jit(solution)/shard_map/scatter-add | solution.py:176
  285.2 11.8 %scatter_custom_fusion.14 = f32[64,1536]{0,1:T(8,128)S(1)} fusion(s32[2048]{0:T(1024)} %bitcast.611, f32[2048,64]{1,0:T(8,128)S(1)} %copy.141, f32[]{:T(128)} %constant.151.clone.1), kind=kCustom, calls=%fused_computation.292 | custom fusion | flops 131072 | bytes 393728 | tf_op jit(solution)/shard_map/scatter-add | solution.py:179
  299.3 11.8 %scatter_custom_fusion.4 = f32[3,1536]{0,1:T(8,128)S(1)} fusion(s32[2048]{0:T(1024)} %bitcast.615, f32[2048,3]{1,0:T(8,128)S(1)} %copy.122, f32[]{:T(128)} %constant.151.clone.1), kind=kCustom, calls=%fused_computation.298 | custom fusion | flops 6144 | bytes 18944 | tf_op jit(solution)/shard_map/scatter-add | solution.py:175
  312.3 11.8 %scatter_custom_fusion.6 = f32[3,1536]{0,1:T(8,128)S(1)} fusion(s32[2048]{0:T(1024)} %bitcast.612, f32[2048,3]{1,0:T(8,128)S(1)} %copy.125, f32[]{:T(128)} %constant.151.clone.1), kind=kCustom, calls=%fused_computation.296 | custom fusion | flops 6144 | bytes 18944 | tf_op jit(solution)/shard_map/scatter-add | solution.py:178
  325.4 149.8 %while.56 = (s32[]{:T(128)}, f32[]{:T(128)}, f32[12,3,512]{2,1,0:T(4,128)S(1)}, f32[12,64,512]{2,1,0:T(8,128)}, f32[12,3,512]{2,1,0:T(4,128)S(1)}, /*index=5*/f3...) while((s32[]{:T(128)}, f32[]{:T(128)}, ...), condition=%wide.region_5.6_spmd, body=%wide.region_0.5_spmd.sunk | while | flops 246594080 | bytes 9616197 | solution.py:79
  476.8 2.3 copy.129
  480.7 2.2 copy.131
  482.9 2.2 copy.118
  485.1 2.2 copy.119
  487.3 33.7 %scatter_custom_fusion.8 = f32[64,2048]{0,1:T(8,128)S(1)} fusion(s32[6144]{0:T(1024)} %bitcast.608, f32[6144,64]{1,0:T(8,128)} %copy.129, f32[]{:T(128)} %constant.151.clone.1), kind=kCustom, calls=%fused_computation.288 | custom fusion | flops 393216 | bytes 524800 | tf_op jit(solution)/shard_map/scatter-add | solution.py:139
  521.0 33.9 %scatter_fusion.5 = f32[64,2048]{0,1:T(8,128)S(1)} fusion(f32[64,2048]{0,1:T(8,128)S(1)} %scatter_custom_fusion.8, s32[6144]{0:T(1024)S(1)} %bitcast.582, f32[6144,64]{1,0:T(8,128)} %copy.131), kind=kCustom, calls=%fused_computation.25 | custom fusion | flops 393216 | bytes 4743168 | tf_op jit(solution)/shard_map/scatter-add | solution.py:141
  554.9 33.7 %scatter_custom_fusion = f32[3,2048]{0,1:T(8,128)S(1)} fusion(s32[6144]{0:T(1024)} %bitcast.609, f32[6144,3]{1,0:T(8,128)} %copy.118, f32[]{:T(128)} %constant.151.clone.1), kind=kCustom, calls=%fused_computation.290 | custom fusion | flops 18432 | bytes 25088 | tf_op jit(solution)/shard_map/scatter-add | solution.py:134
  588.7 33.9 %scatter_fusion = f32[3,2048]{0,1:T(8,128)S(1)} fusion(f32[3,2048]{0,1:T(8,128)S(1)} %scatter_custom_fusion, s32[6144]{0:T(1024)S(1)} %bitcast.583, f32[6144,3]{1,0:T(8,128)} %copy.119), kind=kCustom, calls=%fused_computation.17 | custom fusion | flops 18432 | bytes 245760 | tf_op jit(solution)/shard_map/scatter-add | solution.py:134
  622.6 79.3 %psum.7 = f32[]{:T(128)} all-reduce(f32[]{:T(128)S(6)} %add.332), channel_id=1, replica_groups=mesh['gx'=32,'gy'=8] {'gx','gy'}, use_global_device_ids=true, to_apply=%region_18.19 | all-reduce | flops 1 | bytes 8 | tf_op jit(solution)/shard_map/psum | solution.py:183
  704.1 1.9 copy.149
  706.0 2.4 copy.135
  708.4 2.1 copy.120
  710.5 2.2 copy.121
  712.6 11.9 %scatter_fusion.6 = f32[64,2048]{0,1:T(8,128)S(1)} fusion(f32[64,2048]{0,1:T(8,128)S(1)} %scatter_fusion.5, s32[2048]{0:T(1024)S(1)} %bitcast.596, f32[2048,64]{1,0:T(8,128)S(1)} %copy.133), kind=kCustom, calls=%fused_computation.26 | custom fusion | flops 131072 | bytes 1581056 | tf_op jit(solution)/shard_map/scatter-add | solution.py:158
  724.5 12.2 %scatter_fusion.7 = f32[64,2048]{0,1:T(8,128)S(1)} fusion(f32[64,2048]{0,1:T(8,128)S(1)} %scatter_fusion.6, s32[2048]{0:T(1024)} %bitcast.599, f32[2048,64]{1,0:T(8,128)} %copy.135), kind=kCustom, calls=%fused_computation.27 | custom fusion | flops 131072 | bytes 1581056 | tf_op jit(solution)/shard_map/scatter-add | solution.py:174
  736.8 12.2 %scatter_fusion.1 = f32[3,2048]{0,1:T(8,128)S(1)} fusion(f32[3,2048]{0,1:T(8,128)S(1)} %scatter_fusion, s32[2048]{0:T(1024)S(1)} %bitcast.597, f32[2048,3]{1,0:T(8,128)} %copy.120), kind=kCustom, calls=%fused_computation.18 | custom fusion | flops 6144 | bytes 81920 | tf_op jit(solution)/shard_map/scatter-add | solution.py:157
  749.0 12.2 %scatter_fusion.2 = f32[3,2048]{0,1:T(8,128)S(1)} fusion(f32[3,2048]{0,1:T(8,128)S(1)} %scatter_fusion.1, s32[2048]{0:T(1024)S(1)} %bitcast.600, f32[2048,3]{1,0:T(8,128)} %copy.121), kind=kCustom, calls=%fused_computation.19 | custom fusion | flops 6144 | bytes 81920 | tf_op jit(solution)/shard_map/scatter-add | solution.py:173
  763.0 1.9 copy.127
  764.9 9.1 %scatter_fusion.3 = f32[3,2048]{0,1:T(8,128)S(1)} fusion(f32[3,2048]{0,1:T(8,128)S(1)} %scatter_fusion.2, s32[1536]{0:T(1024)S(1)} %copy-done.27, f32[1536,3]{1,0:T(8,128)S(1)} %copy.124), kind=kCustom, calls=%fused_computation.21 | custom fusion | flops 4608 | bytes 61440 | tf_op jit(solution)/shard_map/scatter-add | solution.py:181
  774.1 9.7 %scatter_fusion.4 = f32[3,2048]{0,1:T(8,128)S(1)} fusion(f32[3,2048]{0,1:T(8,128)S(1)} %scatter_fusion.3, s32[1536]{0:T(1024)S(1)} %copy-done.24, f32[1536,3]{1,0:T(8,128)} %copy.127), kind=kCustom, calls=%fused_computation.23 | custom fusion | flops 4608 | bytes 61440 | tf_op jit(solution)/shard_map/scatter-add | solution.py:181
  787.4 9.1 %scatter_fusion.8 = f32[64,2048]{0,1:T(8,128)S(1)} fusion(f32[64,2048]{0,1:T(8,128)S(1)} %scatter_fusion.7, s32[1536]{0:T(1024)S(1)} %copy-done.28, f32[1536,64]{1,0:T(8,128)S(1)} %copy.139), kind=kCustom, calls=%fused_computation.29 | custom fusion | flops 98304 | bytes 1185792 | tf_op jit(solution)/shard_map/scatter-add | solution.py:182
  796.6 9.1 %scatter_fusion.9 = f32[64,2048]{0,1:T(8,128)S(1)} fusion(f32[64,2048]{0,1:T(8,128)S(1)} %scatter_fusion.8, s32[1536]{0:T(1024)S(1)} %copy-done.25, f32[1536,64]{1,0:T(8,128)S(1)} %copy.143), kind=kCustom, calls=%fused_computation.31 | custom fusion | flops 98304 | bytes 1185792 | tf_op jit(solution)/shard_map/scatter-add | solution.py:182
  (538 shorter events, 222.3 us)
Async XLA Ops:
  0.6 8.2 %copy-start.12 = (bf16[64,2048]{1,0:T(8,128)(2,1)S(1)}, bf16[64,2048]{1,0:T(8,128)(2,1)}, u32[]{:S(2)}) copy-start(bf16[64,2048]{1,0:T(8,128)(2,1)} %param.24) | copy-start | bytes 786436
  2.6 2.9 copy-start.23
  2.6 2.9 copy-start.26
  5.5 157.4 %collective-permute-start = (f32[3,1536]{1,0:T(4,128)S(1)}, f32[3,1536]{1,0:T(4,128)}, u32[]{:S(2)}, u32[]{:S(2)}) collective-permute-start(f32[3,1536]{1,0:T(4,128)S(1)} %copy.99), channel_id=1, source_target_pairs={{0,248},{8,0},{16,8},{24,16},{32,24},{40,32},{48,40},{56,48},{64,5... | collective-permute-start | bytes 55304 | tf_op jit(solution)/shard_map/ppermute | solution.py:14
  13.2 16.9 %copy-start.32 = (s32[4,6144]{1,0:T(4,128)S(1)}, s32[4,6144]{1,0:T(4,128)}, u32[]{:S(2)}) copy-start(s32[4,6144]{1,0:T(4,128)} %param.26) | copy-start | bytes 294916
  13.2 17.1 %copy-start.36 = (s32[4,2048]{1,0:T(4,128)S(1)}, s32[4,2048]{1,0:T(4,128)}, u32[]{:S(2)}) copy-start(s32[4,2048]{1,0:T(4,128)} %param.27) | copy-start | bytes 98308
  13.2 17.2 %copy-start.37 = (s32[4,2048]{1,0:T(4,128)S(1)}, s32[4,2048]{1,0:T(4,128)}, u32[]{:S(2)}) copy-start(s32[4,2048]{1,0:T(4,128)} %param.28) | copy-start | bytes 98308
  13.2 170.2 %collective-permute-start.1 = (bf16[64,1536]{0,1:T(8,128)(2,1)}, bf16[64,1536]{0,1:T(8,128)(2,1)S(1)}, u32[]{:S(2)}, u32[]{:S(2)}) collective-permute-start(bf16[64,1536]{0,1:T(8,128)(2,1)} %bitcast.50), channel_id=1, source_target_pairs={{0,248},{8,0},{16,8},{24,16},{32,24},{40,32},{48,40},{56,48},{64,5... | collective-permute-start | bytes 589832 | tf_op jit(solution)/shard_map/ppermute | solution.py:14
  19.4 11.3 %copy-start.40 = (s32[1,3]{1,0:T(1,128)S(1)}, s32[1,3]{1,0:T(1,128)}, u32[]{:S(2)}) copy-start(s32[1,3]{1,0:T(1,128)} %param.29) | copy-start | bytes 40
  22.9 150.2 %collective-permute-start.2 = (f32[3,1536]{1,0:T(4,128)}, f32[3,1536]{1,0:T(4,128)}, u32[]{:S(2)}, u32[]{:S(2)}) collective-permute-start(f32[3,1536]{1,0:T(4,128)} %copy.109), channel_id=1, source_target_pairs={{0,7},{1,0},{2,1},{3,2},{4,3},{5,4},{6,5},{7,6},{8,15},{9,8},{10,9... | collective-permute-start | bytes 55304 | tf_op jit(solution)/shard_map/ppermute | solution.py:14
  29.5 195.5 %collective-permute-start.3 = (bf16[64,1536]{0,1:T(8,128)(2,1)}, bf16[64,1536]{0,1:T(8,128)(2,1)S(1)}, u32[]{:S(2)}, u32[]{:S(2)}) collective-permute-start(bf16[64,1536]{0,1:T(8,128)(2,1)} %bitcast.70), channel_id=1, source_target_pairs={{0,7},{1,0},{2,1},{3,2},{4,3},{5,4},{6,5},{7,6},{8,15},{9,8},{10,9... | collective-permute-start | bytes 589832 | tf_op jit(solution)/shard_map/ppermute | solution.py:14
  30.1 0.6 copy-start.10
  30.2 46.9 %copy-start.33 = (s32[6144,1]{0,1:T(1,128)}, s32[6144,1]{0,1:T(1,128)S(1)}, u32[]{:S(2)}) copy-start(s32[6144,1]{0,1:T(1,128)S(1)} %get-tuple-element.669) | copy-start | bytes 73732
  30.4 46.7 %copy-start.13 = (s32[2048,1]{0,1:T(1,128)}, s32[2048,1]{0,1:T(1,128)S(1)}, u32[]{:S(2)}) copy-start(s32[2048,1]{0,1:T(1,128)S(1)} %get-tuple-element.673) | copy-start | bytes 24580
  30.4 241.8 %copy-start.39 = (s32[2048,1]{0,1:T(1,128)}, s32[2048,1]{0,1:T(1,128)S(1)}, u32[]{:S(2)}) copy-start(s32[2048,1]{0,1:T(1,128)S(1)} %get-tuple-element.674) | copy-start | bytes 24580
  30.5 46.6 %copy-start.15 = (s32[2048,1]{0,1:T(1,128)}, s32[2048,1]{0,1:T(1,128)S(1)}, u32[]{:S(2)}) copy-start(s32[2048,1]{0,1:T(1,128)S(1)} %get-tuple-element.671) | copy-start | bytes 24580
  30.5 46.6 %copy-start.38 = (s32[2048,1]{0,1:T(1,128)}, s32[2048,1]{0,1:T(1,128)S(1)}, u32[]{:S(2)}) copy-start(s32[2048,1]{0,1:T(1,128)S(1)} %get-tuple-element.672) | copy-start | bytes 24580
  152.4 3.1 copy-start.2
  156.9 3.7 copy-start.6
  159.4 3.3 copy-start.5
  183.3 6.6 copy-start
  183.3 6.6 copy-start.1
  183.3 6.6 copy-start.7
  183.3 6.6 copy-start.8
  183.3 6.6 copy-start.9
  183.3 6.6 copy-start.29
  183.3 6.6 copy-start.35
  183.3 6.6 copy-start.41
  225.0 6.4 copy-start.17
  225.0 6.4 copy-start.18
  225.0 7.4 copy-start.34
  270.2 0.6 copy-start.21
  270.2 2.0 copy-start.42
  270.2 14.0 %copy-start.3 = (f32[4,64,512]{2,1,0:T(8,128)}, f32[4,64,512]{2,1,0:T(8,128)S(1)}, u32[]{:S(2)}) copy-start(f32[4,64,512]{2,1,0:T(8,128)S(1)} %get-tuple-element.358) | copy-start | bytes 1572868
  270.2 14.0 %copy-start.20 = (f32[4,3,512]{2,1,0:T(4,128)}, f32[4,3,512]{2,1,0:T(4,128)S(1)}, u32[]{:S(2)}) copy-start(f32[4,3,512]{2,1,0:T(4,128)S(1)} %get-tuple-element.352) | copy-start | bytes 73732
  270.8 14.0 %copy-start.4 = (f32[4,64,512]{2,1,0:T(8,128)S(1)}, f32[4,64,512]{2,1,0:T(8,128)}, u32[]{:S(2)}) copy-start(f32[4,64,512]{2,1,0:T(8,128)} %get-tuple-element.360) | copy-start | bytes 1572868
  284.5 500.3 %collective-permute-start.6 = (f32[64,1536]{1,0:T(8,128)S(1)}, f32[64,1536]{1,0:T(8,128)}, u32[]{:S(2)}, u32[]{:S(2)}) collective-permute-start(f32[64,1536]{1,0:T(8,128)S(1)} %copy.138), channel_id=1, source_target_pairs={{0,8},{8,16},{16,24},{24,32},{32,40},{40,48},{48,56},{56,64},{64,7... | collective-permute-start | bytes 1179656 | tf_op jit(solution)/shard_map/ppermute | solution.py:14
  284.9 14.1 %copy-start.19 = (f32[4,3,512]{2,1,0:T(4,128)S(1)}, f32[4,3,512]{2,1,0:T(4,128)}, u32[]{:S(2)}) copy-start(f32[4,3,512]{2,1,0:T(4,128)} %copy-done.18) | copy-start | bytes 73732
  298.0 14.0 %copy-start.22 = (f32[4,3,512]{2,1,0:T(4,128)S(1)}, f32[4,3,512]{2,1,0:T(4,128)}, u32[]{:S(2)}) copy-start(f32[4,3,512]{2,1,0:T(4,128)} %copy-done.21) | copy-start | bytes 73732
  298.0 488.1 %collective-permute-start.7 = (f32[64,1536]{1,0:T(8,128)}, f32[64,1536]{1,0:T(8,128)}, u32[]{:S(2)}, u32[]{:S(2)}) collective-permute-start(f32[64,1536]{1,0:T(8,128)} %copy.142), channel_id=1, source_target_pairs={{0,1},{1,2},{2,3},{3,4},{4,5},{5,6},{6,7},{7,0},{8,9},{9,10},{10,1... | collective-permute-start | bytes 1179656 | tf_op jit(solution)/shard_map/ppermute | solution.py:14
  311.1 14.3 %copy-start.30 = (f32[12,3,512]{2,1,0:T(4,128)S(1)}, f32[12,3,512]{2,1,0:T(4,128)}, u32[]{:S(2)}) copy-start(f32[12,3,512]{2,1,0:T(4,128)} %custom-call.32) | copy-start | bytes 221188
  311.1 14.3 %copy-start.31 = (f32[12,3,512]{2,1,0:T(4,128)S(1)}, f32[12,3,512]{2,1,0:T(4,128)}, u32[]{:S(2)}) copy-start(f32[12,3,512]{2,1,0:T(4,128)} %custom-call.34) | copy-start | bytes 221188
  311.1 14.3 %copy-start.43 = (bf16[256,64]{0,1:T(8,128)(2,1)S(1)}, bf16[256,64]{0,1:T(8,128)(2,1)}, u32[]{:S(2)}) copy-start(bf16[256,64]{0,1:T(8,128)(2,1)} %copy-done.42) | copy-start | bytes 98308
  312.0 450.0 %collective-permute-start.4 = (f32[3,1536]{1,0:T(4,128)}, f32[3,1536]{1,0:T(4,128)}, u32[]{:S(2)}, u32[]{:S(2)}) collective-permute-start(f32[3,1536]{1,0:T(4,128)} %copy.123), channel_id=1, source_target_pairs={{0,8},{8,16},{16,24},{24,32},{32,40},{40,48},{48,56},{56,64},{64,7... | collective-permute-start | bytes 55304 | tf_op jit(solution)/shard_map/ppermute | solution.py:14
  325.0 438.0 %collective-permute-start.5 = (f32[3,1536]{1,0:T(4,128)}, f32[3,1536]{1,0:T(4,128)}, u32[]{:S(2)}, u32[]{:S(2)}) collective-permute-start(f32[3,1536]{1,0:T(4,128)} %copy.126), channel_id=1, source_target_pairs={{0,1},{1,2},{2,3},{3,4},{4,5},{5,6},{6,7},{7,0},{8,9},{9,10},{10,1... | collective-permute-start | bytes 55304 | tf_op jit(solution)/shard_map/ppermute | solution.py:14
  485.1 35.9 %copy-start.11 = (s32[6144,1]{0,1:T(1,128)S(1)}, s32[6144,1]{0,1:T(1,128)}, u32[]{:S(2)}) copy-start(s32[6144,1]{0,1:T(1,128)} %copy-done.10) | copy-start | bytes 73732
  706.0 6.7 copy-start.14
  724.5 24.5 %copy-start.16 = (s32[2048,1]{0,1:T(1,128)S(1)}, s32[2048,1]{0,1:T(1,128)}, u32[]{:S(2)}) copy-start(s32[2048,1]{0,1:T(1,128)} %copy-done.15) | copy-start | bytes 24580
  736.8 28.1 %copy-start.27 = (s32[1536]{0:T(1024)S(1)}, s32[1536]{0:T(1024)}, u32[]{:S(2)}) copy-start(s32[1536]{0:T(1024)} %copy-done.26) | copy-start | bytes 18436
  736.8 37.3 %copy-start.24 = (s32[1536]{0:T(1024)S(1)}, s32[1536]{0:T(1024)}, u32[]{:S(2)}) copy-start(s32[1536]{0:T(1024)} %copy-done.23) | copy-start | bytes 18436
  783.9 3.5 copy-start.28
  787.4 9.2 %copy-start.25 = (s32[1536]{0:T(1024)S(1)}, s32[1536]{0:T(1024)}, u32[]{:S(2)}) copy-start(s32[1536]{0:T(1024)} %copy-done.23) | copy-start | bytes 18436
where the time goes:
time: 820 us; the launch traced here: 808 us
  other arithmetic  304 us (37%)
  local copies, waits for them, and re-layouts  234 us (29%)
  matrix products  158 us (19%)
  blocking collectives  79.3 us (10%)
  loops' own time  14.5 us (2%)
  starting transfers between devices  14.3 us (2%)
    psum x1, blocking collectives, on_device(): total = lax.psum(energy_loc + energy_x + energy_y, ('gx', 'gy'))  79.3 us
    scatter-add x2, other arithmetic, on_device(): jnp.zeros((3, atoms), jnp.float32).at[:, source].add(grads[0]).at[:, target]  67.6 us
    scatter-add x2, other arithmetic, on_device(): grad_feat = jnp.zeros((width, atoms), jnp.float32).at[:, source].add(grad...  67.6 us
    dot_general x40, matrix products, pair_energy(): jnp.dot(w_hidden.T, hidden, preferred_element_type=jnp.float32)  60 us
    dot_general x40, matrix products, pair_energy(): jnp.dot(w_dst.T, dst_feat.astype(jnp.bfloat16), preferred_element_type=jn...  29.7 us
    dot_general x40, matrix products, pair_energy(): jnp.dot(w_src.T, src_feat.astype(jnp.bfloat16), preferred_element_type=jn...  27 us
    reshape x18, local copies, waits for them, and re-layouts, from_blocks(): return jnp.moveaxis(array, 0, 1).reshape(array.shape[1], -1)  25.3 us
    gather x1, local copies, waits for them, and re-layouts, on_device(): features[:, target]  22.1 us
  transfers between devices with their start and end apart: 8, of which 0 were waited for; matrix products, arithmetic and copies ran while one was open for 76% of the time, Pallas kernels for 0%

commit v1 on v0

--- a/solution.py
+++ b/solution.py
@@ -180,7 +180,7 @@
     back_pos_y, back_feat_y = shifted((lent_pos_y, lent_feat_y), "gy", 1)
     grad_pos = grad_pos.at[:, list_x].add(back_pos_x).at[:, list_y].add(back_pos_y)
     grad_feat = grad_feat.at[:, list_x].add(back_feat_x).at[:, list_y].add(back_feat_y)
-    total = lax.psum(energy_loc + energy_x + energy_y, ("gx", "gy"))
+    total = jnp.sum(lax.all_gather(energy_loc + energy_x + energy_y, ("gx", "gy")), axis=0)
     atoms_all = atoms * lax.axis_size("gx") * lax.axis_size("gy")
     energy = (total / atoms_all).reshape(1)
     return (energy, -grad_pos, grad_feat)

time: 820 us -> 820 us (level)
    psum x1 -> x0, blocking collectives: 79.3 us -> none  [on_device(): total = lax.psum(energy_loc + energy_x + energy_y, ('gx', 'gy'))]
    unnamed x0 -> x1, blocking collectives: none -> 79.2 us
where the time goes in v1:
time: 820 us; the launch traced here: 809 us
  other arithmetic  305 us (37%)
  local copies, waits for them, and re-layouts  234 us (29%)
  matrix products  158 us (19%)
  blocking collectives  79.2 us (10%)
  loops' own time  14.5 us (2%)
  starting transfers between devices  14.3 us (2%)
    unnamed x1, blocking collectives  79.2 us
    scatter-add x2, other arithmetic, on_device(): jnp.zeros((3, atoms), jnp.float32).at[:, source].add(grads[0]).at[:, target]  67.6 us
    scatter-add x2, other arithmetic, on_device(): grad_feat = jnp.zeros((width, atoms), jnp.float32).at[:, source].add(grad...  67.6 us
    dot_general x40, matrix products, pair_energy(): jnp.dot(w_hidden.T, hidden, preferred_element_type=jnp.float32)  60 us
    dot_general x40, matrix products, pair_energy(): jnp.dot(w_dst.T, dst_feat.astype(jnp.bfloat16), preferred_element_type=jn...  29.7 us
    dot_general x40, matrix products, pair_energy(): jnp.dot(w_src.T, src_feat.astype(jnp.bfloat16), preferred_element_type=jn...  27 us
    reshape x18, local copies, waits for them, and re-layouts, from_blocks(): return jnp.moveaxis(array, 0, 1).reshape(array.shape[1], -1)  25.3 us
    gather x1, local copies, waits for them, and re-layouts, on_device(): features[:, target]  22.1 us
  transfers between devices with their start and end apart: 8, of which 0 were waited for; matrix products, arithmetic and copies ran while one was open for 76% of the time, Pallas kernels for 0%

profile of v1, /device:TPU:1, one launch (start us, length us, event | category | flops | bytes accessed | tf_op | source)
XLA Modules:
  0.0 809.0 jit_solution(3781290517392980810)
XLA Ops:
  2.7 2.6 gather_fusion.4
  5.5 3.3 collective-permute-start
  9.1 4.0 gather_fusion.8
  13.2 6.3 collective-permute-start.1
  19.4 2.6 gather_fusion.10
  22.9 2.6 collective-permute-start.2
  25.5 4.0 gather_fusion.14
  34.0 21.1 %gather_fusion.1 = f32[6144,3]{1,0:T(8,128)} fusion(f32[3,2048]{0,1:T(8,128)S(1)} %copy.90, s32[6144]{0:T(1024)S(1)} %broadcast_clamp_fusion), kind=kCustom, calls=%fused_computation.1 | custom fusion | bytes 172032 | tf_op jit(solution)/shard_map/gather | solution.py:123
  55.0 22.0 %gather_fusion.2 = bf16[6144,64]{1,0:T(8,128)(2,1)} fusion(bf16[64,2048]{0,1:T(8,128)(2,1)S(1)} %copy.94, s32[6144]{0:T(1024)S(1)} %broadcast_clamp_fusion), kind=kCustom, calls=%fused_computation.2 | custom fusion | bytes 1597440 | tf_op jit(solution)/shard_map/gather | solution.py:124
  77.1 20.9 %gather_fusion = f32[6144,3]{1,0:T(8,128)} fusion(f32[3,2048]{0,1:T(8,128)S(1)} %copy.90, s32[6144]{0:T(1024)S(1)} %broadcast_clamp_fusion.1), kind=kCustom, calls=%fused_computation | custom fusion | bytes 172032 | tf_op jit(solution)/shard_map/gather | solution.py:125
  98.0 22.1 %gather_fusion.3 = bf16[6144,64]{1,0:T(8,128)(2,1)} fusion(bf16[64,2048]{0,1:T(8,128)(2,1)S(1)} %copy.94, s32[6144]{0:T(1024)S(1)} %broadcast_clamp_fusion.1), kind=kCustom, calls=%fused_computation.3 | custom fusion | bytes 1597440 | tf_op jit(solution)/shard_map/gather | solution.py:126
  120.1 7.6 gather_fusion.6
  127.6 6.2 gather_fusion.7
  133.8 7.6 gather_fusion.12
  141.4 8.0 gather_fusion.13
  149.4 3.0 copy.91
  152.4 3.1 copy.93
  156.9 2.5 copy.97
  164.0 7.6 gather_fusion.5
  174.2 7.6 gather_fusion.11
  183.4 6.2 gather_fusion.9
  190.0 35.0 %while.57 = (s32[]{:T(128)}, f32[]{:T(128)}, f32[4,3,512]{2,1,0:T(4,128)S(1)}, f32[4,64,512]{2,1,0:T(8,128)S(1)}, f32[4,3,512]{2,1,0:T(4,128)S(1)}, /*index=5*/f...) while((s32[]{:T(128)}, f32[]{:T(128)}, ...), condition=%wide.region_11.12_spmd.clone, body=%wide.region_6.11_spmd.sunk.clone.sunk | while | flops 246597152 | bytes 9618793 | solution.py:79
  191.7 2.0 convolution_bitcast_fusion.14
  200.4 2.0 convolution_bitcast_fusion.14
  202.4 1.6 fusion.381
  209.2 2.0 convolution_bitcast_fusion.14
  211.1 1.6 fusion.381
  217.9 2.0 convolution_bitcast_fusion.14
  225.0 6.2 gather_fusion.15
  232.4 37.8 %while.58 = (s32[]{:T(128)}, f32[]{:T(128)}, f32[4,3,512]{2,1,0:T(4,128)S(1)}, f32[4,64,512]{2,1,0:T(8,128)S(1)}, f32[4,3,512]{2,1,0:T(4,128)S(1)}, /*index=5*/f...) while((s32[]{:T(128)}, f32[]{:T(128)}, ...), condition=%wide.region_17.18_spmd.clone, body=%wide.region_12.17_spmd.sunk.clone.sunk | while | flops 246597152 | bytes 9619301 | solution.py:79
  234.1 2.0 convolution_bitcast_fusion.16
  236.1 1.6 fusion.411
  243.5 2.0 convolution_bitcast_fusion.16
  245.5 1.6 fusion.411
  253.0 2.0 convolution_bitcast_fusion.16
  255.0 1.6 fusion.411
  262.4 2.0 convolution_bitcast_fusion.16
  272.2 12.0 %scatter_custom_fusion.12 = f32[64,1536]{0,1:T(8,128)S(1)} fusion(s32[2048]{0:T(1024)S(1)} %bitcast.615, f32[2048,64]{1,0:T(8,128)} %copy.137, f32[]{:T(128)} %constant.151.clone.1), kind=kCustom, calls=%fused_computation.294 | custom fusion | flops 131072 | bytes 393728 | tf_op jit(solution)/shard_map/scatter-add | solution.py:176
  285.2 11.8 %scatter_custom_fusion.14 = f32[64,1536]{0,1:T(8,128)S(1)} fusion(s32[2048]{0:T(1024)} %bitcast.612, f32[2048,64]{1,0:T(8,128)S(1)} %copy.141, f32[]{:T(128)} %constant.151.clone.1), kind=kCustom, calls=%fused_computation.292 | custom fusion | flops 131072 | bytes 393728 | tf_op jit(solution)/shard_map/scatter-add | solution.py:179
  299.3 11.8 %scatter_custom_fusion.4 = f32[3,1536]{0,1:T(8,128)S(1)} fusion(s32[2048]{0:T(1024)} %bitcast.616, f32[2048,3]{1,0:T(8,128)S(1)} %copy.122, f32[]{:T(128)} %constant.151.clone.1), kind=kCustom, calls=%fused_computation.298 | custom fusion | flops 6144 | bytes 18944 | tf_op jit(solution)/shard_map/scatter-add | solution.py:175
  312.3 11.8 %scatter_custom_fusion.6 = f32[3,1536]{0,1:T(8,128)S(1)} fusion(s32[2048]{0:T(1024)} %bitcast.613, f32[2048,3]{1,0:T(8,128)S(1)} %copy.125, f32[]{:T(128)} %constant.151.clone.1), kind=kCustom, calls=%fused_computation.296 | custom fusion | flops 6144 | bytes 18944 | tf_op jit(solution)/shard_map/scatter-add | solution.py:178
  325.4 149.8 %while.56 = (s32[]{:T(128)}, f32[]{:T(128)}, f32[12,3,512]{2,1,0:T(4,128)S(1)}, f32[12,64,512]{2,1,0:T(8,128)}, f32[12,3,512]{2,1,0:T(4,128)S(1)}, /*index=5*/f3...) while((s32[]{:T(128)}, f32[]{:T(128)}, ...), condition=%wide.region_5.6_spmd, body=%wide.region_0.5_spmd.sunk | while | flops 246594080 | bytes 9616197 | solution.py:79
  476.8 2.3 copy.129
  480.7 2.2 copy.131
  482.9 2.2 copy.118
  485.1 2.2 copy.119
  487.3 33.7 %scatter_custom_fusion.8 = f32[64,2048]{0,1:T(8,128)S(1)} fusion(s32[6144]{0:T(1024)} %bitcast.609, f32[6144,64]{1,0:T(8,128)} %copy.129, f32[]{:T(128)} %constant.151.clone.1), kind=kCustom, calls=%fused_computation.288 | custom fusion | flops 393216 | bytes 524800 | tf_op jit(solution)/shard_map/scatter-add | solution.py:139
  521.0 33.9 %scatter_fusion.5 = f32[64,2048]{0,1:T(8,128)S(1)} fusion(f32[64,2048]{0,1:T(8,128)S(1)} %scatter_custom_fusion.8, s32[6144]{0:T(1024)S(1)} %bitcast.583, f32[6144,64]{1,0:T(8,128)} %copy.131), kind=kCustom, calls=%fused_computation.25 | custom fusion | flops 393216 | bytes 4743168 | tf_op jit(solution)/shard_map/scatter-add | solution.py:141
  554.9 33.7 %scatter_custom_fusion = f32[3,2048]{0,1:T(8,128)S(1)} fusion(s32[6144]{0:T(1024)} %bitcast.610, f32[6144,3]{1,0:T(8,128)} %copy.118, f32[]{:T(128)} %constant.151.clone.1), kind=kCustom, calls=%fused_computation.290 | custom fusion | flops 18432 | bytes 25088 | tf_op jit(solution)/shard_map/scatter-add | solution.py:134
  588.7 33.9 %scatter_fusion = f32[3,2048]{0,1:T(8,128)S(1)} fusion(f32[3,2048]{0,1:T(8,128)S(1)} %scatter_custom_fusion, s32[6144]{0:T(1024)S(1)} %bitcast.584, f32[6144,3]{1,0:T(8,128)} %copy.119), kind=kCustom, calls=%fused_computation.17 | custom fusion | flops 18432 | bytes 245760 | tf_op jit(solution)/shard_map/scatter-add | solution.py:134
  624.8 1.9 copy.149
  626.7 2.4 copy.135
  629.1 2.1 copy.120
  631.2 2.2 copy.121
  633.3 12.0 %scatter_fusion.6 = f32[64,2048]{0,1:T(8,128)S(1)} fusion(f32[64,2048]{0,1:T(8,128)S(1)} %scatter_fusion.5, s32[2048]{0:T(1024)S(1)} %bitcast.597, f32[2048,64]{1,0:T(8,128)S(1)} %copy.133), kind=kCustom, calls=%fused_computation.26 | custom fusion | flops 131072 | bytes 1581056 | tf_op jit(solution)/shard_map/scatter-add | solution.py:158
  645.4 12.2 %scatter_fusion.7 = f32[64,2048]{0,1:T(8,128)S(1)} fusion(f32[64,2048]{0,1:T(8,128)S(1)} %scatter_fusion.6, s32[2048]{0:T(1024)} %bitcast.600, f32[2048,64]{1,0:T(8,128)} %copy.135), kind=kCustom, calls=%fused_computation.27 | custom fusion | flops 131072 | bytes 1581056 | tf_op jit(solution)/shard_map/scatter-add | solution.py:174
  657.7 12.2 %scatter_fusion.1 = f32[3,2048]{0,1:T(8,128)S(1)} fusion(f32[3,2048]{0,1:T(8,128)S(1)} %scatter_fusion, s32[2048]{0:T(1024)S(1)} %bitcast.598, f32[2048,3]{1,0:T(8,128)} %copy.120), kind=kCustom, calls=%fused_computation.18 | custom fusion | flops 6144 | bytes 81920 | tf_op jit(solution)/shard_map/scatter-add | solution.py:157
  669.9 12.2 %scatter_fusion.2 = f32[3,2048]{0,1:T(8,128)S(1)} fusion(f32[3,2048]{0,1:T(8,128)S(1)} %scatter_fusion.1, s32[2048]{0:T(1024)S(1)} %bitcast.601, f32[2048,3]{1,0:T(8,128)} %copy.121), kind=kCustom, calls=%fused_computation.19 | custom fusion | flops 6144 | bytes 81920 | tf_op jit(solution)/shard_map/scatter-add | solution.py:173
  682.3 79.2 %all-reduce = f32[256]{0:T(256)S(1)} all-reduce(f32[256]{0:T(256)S(1)} %dynamic-update-slice), channel_id=1, replica_groups=mesh['gx'=32,'gy'=8] {'gx','gy'}, use_global_device_ids=true, to_apply=%add | all-reduce | flops 256 | bytes 2048
  763.7 1.9 copy.127
  765.7 9.1 %scatter_fusion.3 = f32[3,2048]{0,1:T(8,128)S(1)} fusion(f32[3,2048]{0,1:T(8,128)S(1)} %scatter_fusion.2, s32[1536]{0:T(1024)S(1)} %copy-done.27, f32[1536,3]{1,0:T(8,128)S(1)} %copy.124), kind=kCustom, calls=%fused_computation.21 | custom fusion | flops 4608 | bytes 61440 | tf_op jit(solution)/shard_map/scatter-add | solution.py:181
  774.8 9.7 %scatter_fusion.4 = f32[3,2048]{0,1:T(8,128)S(1)} fusion(f32[3,2048]{0,1:T(8,128)S(1)} %scatter_fusion.3, s32[1536]{0:T(1024)S(1)} %copy-done.24, f32[1536,3]{1,0:T(8,128)} %copy.127), kind=kCustom, calls=%fused_computation.23 | custom fusion | flops 4608 | bytes 61440 | tf_op jit(solution)/shard_map/scatter-add | solution.py:181
  788.2 9.1 %scatter_fusion.8 = f32[64,2048]{0,1:T(8,128)S(1)} fusion(f32[64,2048]{0,1:T(8,128)S(1)} %scatter_fusion.7, s32[1536]{0:T(1024)S(1)} %copy-done.28, f32[1536,64]{1,0:T(8,128)S(1)} %copy.139), kind=kCustom, calls=%fused_computation.29 | custom fusion | flops 98304 | bytes 1185792 | tf_op jit(solution)/shard_map/scatter-add | solution.py:182
  797.3 9.1 %scatter_fusion.9 = f32[64,2048]{0,1:T(8,128)S(1)} fusion(f32[64,2048]{0,1:T(8,128)S(1)} %scatter_fusion.8, s32[1536]{0:T(1024)S(1)} %copy-done.25, f32[1536,64]{1,0:T(8,128)S(1)} %copy.143), kind=kCustom, calls=%fused_computation.31 | custom fusion | flops 98304 | bytes 1185792 | tf_op jit(solution)/shard_map/scatter-add | solution.py:182
  (541 shorter events, 223.0 us)
Async XLA Ops:
  0.6 8.2 %copy-start.12 = (bf16[64,2048]{1,0:T(8,128)(2,1)S(1)}, bf16[64,2048]{1,0:T(8,128)(2,1)}, u32[]{:S(2)}) copy-start(bf16[64,2048]{1,0:T(8,128)(2,1)} %param.24) | copy-start | bytes 786436
  2.6 2.9 copy-start.23
  2.6 2.9 copy-start.26
  5.5 157.4 %collective-permute-start = (f32[3,1536]{1,0:T(4,128)S(1)}, f32[3,1536]{1,0:T(4,128)}, u32[]{:S(2)}, u32[]{:S(2)}) collective-permute-start(f32[3,1536]{1,0:T(4,128)S(1)} %copy.99), channel_id=1, source_target_pairs={{0,248},{8,0},{16,8},{24,16},{32,24},{40,32},{48,40},{56,48},{64,5... | collective-permute-start | bytes 55304 | tf_op jit(solution)/shard_map/ppermute | solution.py:14
  13.2 16.9 %copy-start.32 = (s32[4,6144]{1,0:T(4,128)S(1)}, s32[4,6144]{1,0:T(4,128)}, u32[]{:S(2)}) copy-start(s32[4,6144]{1,0:T(4,128)} %param.26) | copy-start | bytes 294916
  13.2 17.1 %copy-start.36 = (s32[4,2048]{1,0:T(4,128)S(1)}, s32[4,2048]{1,0:T(4,128)}, u32[]{:S(2)}) copy-start(s32[4,2048]{1,0:T(4,128)} %param.27) | copy-start | bytes 98308
  13.2 17.2 %copy-start.37 = (s32[4,2048]{1,0:T(4,128)S(1)}, s32[4,2048]{1,0:T(4,128)}, u32[]{:S(2)}) copy-start(s32[4,2048]{1,0:T(4,128)} %param.28) | copy-start | bytes 98308
  13.2 170.2 %collective-permute-start.1 = (bf16[64,1536]{0,1:T(8,128)(2,1)}, bf16[64,1536]{0,1:T(8,128)(2,1)S(1)}, u32[]{:S(2)}, u32[]{:S(2)}) collective-permute-start(bf16[64,1536]{0,1:T(8,128)(2,1)} %bitcast.50), channel_id=1, source_target_pairs={{0,248},{8,0},{16,8},{24,16},{32,24},{40,32},{48,40},{56,48},{64,5... | collective-permute-start | bytes 589832 | tf_op jit(solution)/shard_map/ppermute | solution.py:14
  19.4 11.3 %copy-start.40 = (s32[1,3]{1,0:T(1,128)S(1)}, s32[1,3]{1,0:T(1,128)}, u32[]{:S(2)}) copy-start(s32[1,3]{1,0:T(1,128)} %param.29) | copy-start | bytes 40
  22.9 150.2 %collective-permute-start.2 = (f32[3,1536]{1,0:T(4,128)}, f32[3,1536]{1,0:T(4,128)}, u32[]{:S(2)}, u32[]{:S(2)}) collective-permute-start(f32[3,1536]{1,0:T(4,128)} %copy.109), channel_id=1, source_target_pairs={{0,7},{1,0},{2,1},{3,2},{4,3},{5,4},{6,5},{7,6},{8,15},{9,8},{10,9... | collective-permute-start | bytes 55304 | tf_op jit(solution)/shard_map/ppermute | solution.py:14
  29.5 195.5 %collective-permute-start.3 = (bf16[64,1536]{0,1:T(8,128)(2,1)}, bf16[64,1536]{0,1:T(8,128)(2,1)S(1)}, u32[]{:S(2)}, u32[]{:S(2)}) collective-permute-start(bf16[64,1536]{0,1:T(8,128)(2,1)} %bitcast.70), channel_id=1, source_target_pairs={{0,7},{1,0},{2,1},{3,2},{4,3},{5,4},{6,5},{7,6},{8,15},{9,8},{10,9... | collective-permute-start | bytes 589832 | tf_op jit(solution)/shard_map/ppermute | solution.py:14
  30.1 0.6 copy-start.10
  30.2 46.9 %copy-start.33 = (s32[6144,1]{0,1:T(1,128)}, s32[6144,1]{0,1:T(1,128)S(1)}, u32[]{:S(2)}) copy-start(s32[6144,1]{0,1:T(1,128)S(1)} %get-tuple-element.669) | copy-start | bytes 73732
  30.4 46.7 %copy-start.13 = (s32[2048,1]{0,1:T(1,128)}, s32[2048,1]{0,1:T(1,128)S(1)}, u32[]{:S(2)}) copy-start(s32[2048,1]{0,1:T(1,128)S(1)} %get-tuple-element.673) | copy-start | bytes 24580
  30.4 241.8 %copy-start.39 = (s32[2048,1]{0,1:T(1,128)}, s32[2048,1]{0,1:T(1,128)S(1)}, u32[]{:S(2)}) copy-start(s32[2048,1]{0,1:T(1,128)S(1)} %get-tuple-element.674) | copy-start | bytes 24580
  30.5 46.6 %copy-start.15 = (s32[2048,1]{0,1:T(1,128)}, s32[2048,1]{0,1:T(1,128)S(1)}, u32[]{:S(2)}) copy-start(s32[2048,1]{0,1:T(1,128)S(1)} %get-tuple-element.671) | copy-start | bytes 24580
  30.5 46.6 %copy-start.38 = (s32[2048,1]{0,1:T(1,128)}, s32[2048,1]{0,1:T(1,128)S(1)}, u32[]{:S(2)}) copy-start(s32[2048,1]{0,1:T(1,128)S(1)} %get-tuple-element.672) | copy-start | bytes 24580
  152.4 3.1 copy-start.2
  156.9 3.7 copy-start.6
  159.4 3.3 copy-start.5
  183.3 6.6 copy-start
  183.3 6.6 copy-start.1
  183.3 6.6 copy-start.7
  183.3 6.6 copy-start.8
  183.3 6.6 copy-start.9
  183.3 6.6 copy-start.29
  183.3 6.6 copy-start.35
  183.3 6.6 copy-start.41
  225.0 6.4 copy-start.17
  225.0 6.4 copy-start.18
  225.0 7.4 copy-start.34
  270.2 0.6 copy-start.21
  270.2 2.0 copy-start.42
  270.2 14.0 %copy-start.3 = (f32[4,64,512]{2,1,0:T(8,128)}, f32[4,64,512]{2,1,0:T(8,128)S(1)}, u32[]{:S(2)}) copy-start(f32[4,64,512]{2,1,0:T(8,128)S(1)} %get-tuple-element.358) | copy-start | bytes 1572868
  270.2 14.0 %copy-start.20 = (f32[4,3,512]{2,1,0:T(4,128)}, f32[4,3,512]{2,1,0:T(4,128)S(1)}, u32[]{:S(2)}) copy-start(f32[4,3,512]{2,1,0:T(4,128)S(1)} %get-tuple-element.352) | copy-start | bytes 73732
  270.8 14.0 %copy-start.4 = (f32[4,64,512]{2,1,0:T(8,128)S(1)}, f32[4,64,512]{2,1,0:T(8,128)}, u32[]{:S(2)}) copy-start(f32[4,64,512]{2,1,0:T(8,128)} %get-tuple-element.360) | copy-start | bytes 1572868
  284.5 501.1 %collective-permute-start.6 = (f32[64,1536]{1,0:T(8,128)S(1)}, f32[64,1536]{1,0:T(8,128)}, u32[]{:S(2)}, u32[]{:S(2)}) collective-permute-start(f32[64,1536]{1,0:T(8,128)S(1)} %copy.138), channel_id=1, source_target_pairs={{0,8},{8,16},{16,24},{24,32},{32,40},{40,48},{48,56},{56,64},{64,7... | collective-permute-start | bytes 1179656 | tf_op jit(solution)/shard_map/ppermute | solution.py:14
  284.9 14.1 %copy-start.19 = (f32[4,3,512]{2,1,0:T(4,128)S(1)}, f32[4,3,512]{2,1,0:T(4,128)}, u32[]{:S(2)}) copy-start(f32[4,3,512]{2,1,0:T(4,128)} %copy-done.18) | copy-start | bytes 73732
  298.0 14.0 %copy-start.22 = (f32[4,3,512]{2,1,0:T(4,128)S(1)}, f32[4,3,512]{2,1,0:T(4,128)}, u32[]{:S(2)}) copy-start(f32[4,3,512]{2,1,0:T(4,128)} %copy-done.21) | copy-start | bytes 73732
  298.0 488.9 %collective-permute-start.7 = (f32[64,1536]{1,0:T(8,128)}, f32[64,1536]{1,0:T(8,128)}, u32[]{:S(2)}, u32[]{:S(2)}) collective-permute-start(f32[64,1536]{1,0:T(8,128)} %copy.142), channel_id=1, source_target_pairs={{0,1},{1,2},{2,3},{3,4},{4,5},{5,6},{6,7},{7,0},{8,9},{9,10},{10,1... | collective-permute-start | bytes 1179656 | tf_op jit(solution)/shard_map/ppermute | solution.py:14
  311.1 14.3 %copy-start.30 = (f32[12,3,512]{2,1,0:T(4,128)S(1)}, f32[12,3,512]{2,1,0:T(4,128)}, u32[]{:S(2)}) copy-start(f32[12,3,512]{2,1,0:T(4,128)} %custom-call.32) | copy-start | bytes 221188
  311.1 14.3 %copy-start.31 = (f32[12,3,512]{2,1,0:T(4,128)S(1)}, f32[12,3,512]{2,1,0:T(4,128)}, u32[]{:S(2)}) copy-start(f32[12,3,512]{2,1,0:T(4,128)} %custom-call.34) | copy-start | bytes 221188
  311.1 14.3 %copy-start.43 = (bf16[256,64]{0,1:T(8,128)(2,1)S(1)}, bf16[256,64]{0,1:T(8,128)(2,1)}, u32[]{:S(2)}) copy-start(bf16[256,64]{0,1:T(8,128)(2,1)} %copy-done.42) | copy-start | bytes 98308
  312.0 450.7 %collective-permute-start.4 = (f32[3,1536]{1,0:T(4,128)}, f32[3,1536]{1,0:T(4,128)}, u32[]{:S(2)}, u32[]{:S(2)}) collective-permute-start(f32[3,1536]{1,0:T(4,128)} %copy.123), channel_id=1, source_target_pairs={{0,8},{8,16},{16,24},{24,32},{32,40},{40,48},{48,56},{56,64},{64,7... | collective-permute-start | bytes 55304 | tf_op jit(solution)/shard_map/ppermute | solution.py:14
  325.0 438.7 %collective-permute-start.5 = (f32[3,1536]{1,0:T(4,128)}, f32[3,1536]{1,0:T(4,128)}, u32[]{:S(2)}, u32[]{:S(2)}) collective-permute-start(f32[3,1536]{1,0:T(4,128)} %copy.126), channel_id=1, source_target_pairs={{0,1},{1,2},{2,3},{3,4},{4,5},{5,6},{6,7},{7,0},{8,9},{9,10},{10,1... | collective-permute-start | bytes 55304 | tf_op jit(solution)/shard_map/ppermute | solution.py:14
  485.1 36.0 %copy-start.11 = (s32[6144,1]{0,1:T(1,128)S(1)}, s32[6144,1]{0,1:T(1,128)}, u32[]{:S(2)}) copy-start(s32[6144,1]{0,1:T(1,128)} %copy-done.10) | copy-start | bytes 73732
  626.7 6.7 copy-start.14
  645.4 24.5 %copy-start.16 = (s32[2048,1]{0,1:T(1,128)S(1)}, s32[2048,1]{0,1:T(1,128)}, u32[]{:S(2)}) copy-start(s32[2048,1]{0,1:T(1,128)} %copy-done.15) | copy-start | bytes 24580
  657.6 108.0 %copy-start.27 = (s32[1536]{0:T(1024)S(1)}, s32[1536]{0:T(1024)}, u32[]{:S(2)}) copy-start(s32[1536]{0:T(1024)} %copy-done.26) | copy-start | bytes 18436
  657.6 117.2 %copy-start.24 = (s32[1536]{0:T(1024)S(1)}, s32[1536]{0:T(1024)}, u32[]{:S(2)}) copy-start(s32[1536]{0:T(1024)} %copy-done.23) | copy-start | bytes 18436
  784.6 3.5 copy-start.28
  788.2 9.2 %copy-start.25 = (s32[1536]{0:T(1024)S(1)}, s32[1536]{0:T(1024)}, u32[]{:S(2)}) copy-start(s32[1536]{0:T(1024)} %copy-done.23) | copy-start | bytes 18436
